TPU v7x, 512 devices: a whole 4x8x8 slice. The times are simulated.
512 devices in a mesh: blk: 32 (over y, x), col: 16 (over z, core).
Axes of the slice: x: 4, y: 8, z: 8, core: 2. Of those that a mesh axis runs over, the one named last changes fastest.
Arguments:
- visit_cov: bfloat16 [32768, 128], P('blk'), may hold values from -6 to 6
- tumor_size: bfloat16 [32768], P('blk'), may hold values from -6 to 6
- visit_weight: bfloat16 [32768], P('blk'), may hold values from 0.5 to 2
- visit_owner: int32 [32768, 1], P('blk'), may hold values from 0 to 31; in each aligned block of 1024 rows (0 to 1023, 1024 to 2047, ...) at most 64 rows name the same one
- visit_patient: int32 [32768], P('blk'), may hold values from 0 to 127
- inducing_freq: bfloat16 [128, 2048], P(None, 'col'), may hold values from -1.5 to 1.5
- inducing_phase: bfloat16 [2048], P('col'), may hold values from -3.140625 to 3.140625
- node_cov: bfloat16 [4096, 16, 128], P('blk'), may hold values from -6 to 6
- event_time: float32 [4096], P('blk'), may hold values from 0.2 to 2
- event_flag: int32 [4096], P('blk'), may hold values 0 or 1
Outputs:
- loglik: float32 [4096], P('blk')
- mean_weights: float32 [2048], P('col')
Inputs may be any that keep to these rules, and one draw needn't show every extreme that they name: `visit_owner`: among the visits entering one index of blk, no owner is named more than 64 times, a bound that some block reaches.
All inputs are finite; a program needn't handle non-finite values. No bound on the sum of `event_flag` on one device may be relied on, other than what follows from the above.
Results may differ from a plain program's by a relative error of at most 0.003.
Values may be sent and summed in bfloat16 or wider, within the bound.
No kernel may reach another device: no remote copies, remote signals or barrier semaphores. Data moves between devices by JAX's collectives and lax.ppermute only.
A program may use at most 64 MiB of HBM per device.

v0:
```python
import math
import jax
import jax.numpy as jnp
from jax import lax
from jax.sharding import PartitionSpec as P

ITERS = 3
SQRT_TWO = math.sqrt(2.0)
LOG_SHAPE = math.log(1.5)
LINK = 0.4


def features(covariates, frequency, phases):
    angles = jnp.dot(covariates, frequency, preferred_element_type=jnp.float32) + phases.astype(
        jnp.float32
    )
    return (SQRT_TWO * jnp.cos(angles)).astype(jnp.bfloat16)


def norm_of(vector):
    return lax.psum(jnp.sum(vector * vector), "col")


def on_device(
    visit_cov,
    tumor_size,
    visit_weight,
    visit_owner,
    visit_patient,
    inducing_freq,
    inducing_phase,
    node_cov,
    event_time,
    event_flag,
):
    blocks = lax.axis_size("blk")
    visits_here = visit_cov.shape[0]
    width_in = visit_cov.shape[1]
    total_visits = visits_here * blocks
    owners = visit_owner[:, 0]
    owner_table = (owners[:, None] == jnp.arange(blocks, dtype=jnp.int32)[None, :]).astype(
        jnp.int32
    )
    capacity = 2 * visits_here // blocks
    slots = blocks * capacity
    ranking = jnp.cumsum(owner_table, axis=0) - 1
    target = owners * capacity + jnp.sum(owner_table * ranking, axis=1)
    cov_buffer = (
        jnp.zeros((slots, width_in), jnp.bfloat16)
        .at[target]
        .set(visit_cov)
        .reshape(blocks, capacity, width_in)
    )
    packed = jnp.stack([visit_weight, tumor_size, visit_patient.astype(jnp.bfloat16)], axis=1)
    val_buffer = (
        jnp.zeros((slots, 3), jnp.bfloat16)
        .at[target]
        .set(packed)
        .reshape(blocks, capacity, 3)
        .transpose(0, 2, 1)
    )
    cov_in, val_in = (
        lax.all_to_all(cov_buffer, "blk", split_axis=0, concat_axis=0, tiled=True),
        lax.all_to_all(val_buffer, "blk", split_axis=0, concat_axis=0, tiled=True),
    )
    cov_in = cov_in.reshape(slots, width_in)
    weight_in = val_in[:, 0, :].reshape(slots).astype(jnp.float32)
    size_in = val_in[:, 1, :].reshape(slots).astype(jnp.float32)
    patient_in = val_in[:, 2, :].reshape(slots).astype(jnp.int32)
    row_count = cov_in.shape[0]
    phi_local = features(cov_in, inducing_freq, inducing_phase)
    phi_wide = phi_local.astype(jnp.float32)
    rhs_local = jnp.dot(weight_in * size_in, phi_wide, precision=lax.Precision.HIGHEST)
    local_cols = inducing_freq.shape[1]
    inducing = local_cols * lax.axis_size("col")
    freq_all, phase_all = (
        lax.all_gather(inducing_freq, "col", axis=1, tiled=True),
        lax.all_gather(inducing_phase, "col", axis=0, tiled=True),
    )
    step_rows = min(512, row_count)

    def add_block(index, gram):
        first = index * step_rows
        rows_cov = lax.dynamic_slice_in_dim(cov_in, first, step_rows, 0)
        rows_weight = lax.dynamic_slice_in_dim(weight_in, first, step_rows, 0)
        rows_phi = lax.dynamic_slice_in_dim(phi_local, first, step_rows, 0)
        full_phi = features(rows_cov, freq_all, phase_all)
        weighted = (rows_weight[:, None] * full_phi.astype(jnp.float32)).astype(jnp.bfloat16)
        return gram + lax.dot_general(
            weighted, rows_phi, (((0,), (0,)), ((), ())), preferred_element_type=jnp.float32
        )

    gram = lax.fori_loop(
        0, row_count // step_rows, add_block, jnp.zeros((inducing, local_cols), jnp.float32)
    )
    gram, rhs = lax.psum((gram, rhs_local), "blk")
    gram = gram / total_visits
    rhs = rhs / math.sqrt(total_visits)
    solution = jnp.zeros((local_cols,), jnp.float32)
    residual = rhs
    direction = rhs
    norm_now = norm_of(residual)
    for turn in range(ITERS):
        whole = lax.all_gather(direction, "col", axis=0, tiled=True)
        image = direction + jnp.dot(whole, gram, precision=lax.Precision.HIGHEST)
        alpha = norm_now / lax.psum(jnp.sum(direction * image), "col")
        solution = solution + alpha * direction
        residual = residual - alpha * image
        norm_next = norm_of(residual)
        direction = residual + norm_next / norm_now * direction
        norm_now = norm_next
    nodes_flat = node_cov.reshape(-1, width_in)
    node_phi = features(nodes_flat, inducing_freq, inducing_phase)
    fit_part = jnp.dot(phi_wide, solution, precision=lax.Precision.HIGHEST)
    node_part = jnp.dot(node_phi.astype(jnp.float32), solution, precision=lax.Precision.HIGHEST)
    fitted, node_value = lax.psum((fit_part, node_part), "col")
    fitted = fitted / math.sqrt(inducing)
    node_value = node_value / math.sqrt(inducing)
    patients_here = event_time.shape[0]
    nodes_count = node_cov.shape[1]
    patient_table = (
        patient_in[:, None] == jnp.arange(patients_here, dtype=jnp.int32)[None, :]
    ).astype(jnp.float32)
    residual_term = weight_in * (size_in - fitted)
    numer = jnp.dot(residual_term, patient_table, precision=lax.Precision.HIGHEST)
    denom = 1.0 + jnp.dot(weight_in, patient_table, precision=lax.Precision.HIGHEST)
    effect = numer / denom
    grid = (
        event_time[:, None]
        * (jnp.arange(nodes_count).astype(jnp.float32)[None, :] + 1.0)
        / nodes_count
    )
    eta = (
        LOG_SHAPE
        + 0.5 * jnp.log(grid)
        + LINK * (node_value.reshape(patients_here, nodes_count) + effect[:, None])
    )
    loglik = event_flag.astype(jnp.float32) * eta[:, -1] - event_time / nodes_count * jnp.sum(
        jnp.exp(eta), axis=1
    )
    return (loglik, solution)


def solution(mesh):
    in_specs = (
        P("blk", None),
        P("blk"),
        P("blk"),
        P("blk", None),
        P("blk"),
        P(None, "col"),
        P("col"),
        P("blk", None, None),
        P("blk"),
        P("blk"),
    )
    out_specs = (P("blk"), P("col"))
    return jax.shard_map(
        on_device, mesh=mesh, in_specs=in_specs, out_specs=out_specs, check_vma=False
    )
```

profile of v0, /device:TPU:16, one launch (start us, length us, event | category | flops | bytes accessed | tf_op | source)
XLA Modules:
  0.0 532.7 jit_solution(2748140927083613573)
XLA Ops:
  7.2 0.0 copy-start
  7.2 0.7 fusion.35
  8.0 9.0 %reduce-window.6 = s32[32,8,128]{2,1,0:T(8,128)S(1)} reduce-window(s32[32,8,128]{2,1,0:T(8,128)S(1)} %fusion.35, s32[]{:T(128)} %constant.72.clone.1), window={size=1x1x128 pad=0_0x0_0x127_0}, to_apply=%region_0.0 | reduce-window | flops 4161536 | bytes 262148 | tf_op jit(solution)/shard_map/reduce-window
  17.0 0.1 slice.24
  17.1 0.1 copy.22
  17.3 0.1 copy.23
  17.3 0.1 add_add_fusion
  17.6 0.2 copy.24
  17.8 3.3 scatter_custom_fusion
  21.2 0.0 copy-start.10
  21.2 0.9 copy.25
  22.1 10.1 %all-to-all-start = ((bf16[32,3,64]{2,1,0:T(4,128)(2,1)}), bf16[32,3,64]{2,1,0:T(4,128)(2,1)S(1)}, u32[]{:S(2)}, u32[]{:S(2)}) async-start(bf16[32,3,64]{2,1,0:T(4,128)(2,1)} %bitcast.8), calls=%async_computation | async-start | bytes 65536 | tf_op jit(solution)/shard_map/all_to_all | solution.py:64
  32.1 4.3 scatter_custom_fusion.1
  36.5 3.5 all-to-all-done
  40.0 6.2 %all-to-all-start.1 = ((bf16[32,64,128]{2,1,0:T(8,128)(2,1)}), bf16[32,64,128]{2,1,0:T(8,128)(2,1)S(1)}, u32[]{:S(2)}, u32[]{:S(2)}) async-start(bf16[32,64,128]{2,1,0:T(8,128)(2,1)} %bitcast.10), calls=%async_computation.1 | async-start | bytes 1048576 | tf_op jit(solution)/shard_map/all_to_all | solution.py:63
  46.3 0.0 all-reduce.4.cloned.1.call-start
  46.3 23.1 %all-gather.1 = bf16[16,1,128]{2,1,0:T(2,128)(2,1)S(1)} all-gather(bf16[1,1,128]{2,1,0:T(2,128)(2,1)S(1)} %bitcast.121), channel_id=1, replica_groups=mesh['blk'=32,'col'=16] {'col'}, dimensions={0}, use_global_device_ids=true | all-gather | bytes 4352 | tf_op jit(solution)/shard_map/all_gather | solution.py:78
  69.4 15.9 %all_gather.16 = bf16[128,2048]{1,0:T(8,128)(2,1)S(1)} all-gather(bf16[128,128]{1,0:T(8,128)(2,1)S(1)} %copy-done.4), channel_id=1, replica_groups=mesh['blk'=32,'col'=16] {'col'}, dimensions={1}, use_global_device_ids=true | all-gather | bytes 557056 | tf_op jit(solution)/shard_map/all_gather | solution.py:77
  85.3 0.1 slice_reduce_fusion
  85.4 0.1 reshape_squeeze.2
  85.5 3.9 fusion.11
  89.3 61.9 %while.14 = (s32[]{:T(128)}, f32[2048,128]{1,0:T(8,128)S(1)}, f32[2048]{0:T(1024)S(1)}, bf16[2048,128]{1,0:T(8,128)(2,1)S(1)}, bf16[128,2048]{1,0:T(8,128)(2,1)S...) while((s32[]{:T(128)}, f32[2048,128]{1,0:T(8,128)S(1)}, ...), condition=%wide.region_9.10_spmd.clone, body=%wide.region_8.9_spmd.clone.sunk | while | flops 543688704 | bytes 2911912 | solution.py:93
  89.5 0.1 dynamic_slice.34
  89.6 15.2 %convolution_add_fusion.4 = f32[2048,128]{1,0:T(8,128)S(1)} fusion(bf16[128,2048]{1,0:T(8,128)(2,1)S(1)} %get-tuple-element.249, f32[2048]{0:T(1024)S(1)} %convert_element_type.131, f32[512]{0:T(512)S(1)} %dynamic_slice.34, f32[2048,128]{1,0:T(8,128)S(1)} %get-tuple-element.235, pred[]{:T(512)S(6)} %compare.3, ...), kind=kOutput, calls=%fused_computation.4.clone.1 | convolution fusion | flops 543686656 | bytes 2895360 | tf_op jit(solution)/shard_map/while/body/eval_jaxpr/dot_general | solution.py:89
  104.9 0.1 dynamic_slice.34
  105.0 15.3 %convolution_add_fusion.4 = f32[2048,128]{1,0:T(8,128)S(1)} fusion(bf16[128,2048]{1,0:T(8,128)(2,1)S(1)} %get-tuple-element.249, f32[2048]{0:T(1024)S(1)} %convert_element_type.131, f32[512]{0:T(512)S(1)} %dynamic_slice.34, f32[2048,128]{1,0:T(8,128)S(1)} %get-tuple-element.235, pred[]{:T(512)S(6)} %compare.3, ...), kind=kOutput, calls=%fused_computation.4.clone.1 | convolution fusion | flops 543686656 | bytes 2895360 | tf_op jit(solution)/shard_map/while/body/eval_jaxpr/dot_general | solution.py:89
  120.3 0.1 dynamic_slice.34
  120.3 15.3 %convolution_add_fusion.4 = f32[2048,128]{1,0:T(8,128)S(1)} fusion(bf16[128,2048]{1,0:T(8,128)(2,1)S(1)} %get-tuple-element.249, f32[2048]{0:T(1024)S(1)} %convert_element_type.131, f32[512]{0:T(512)S(1)} %dynamic_slice.34, f32[2048,128]{1,0:T(8,128)S(1)} %get-tuple-element.235, pred[]{:T(512)S(6)} %compare.3, ...), kind=kOutput, calls=%fused_computation.4.clone.1 | convolution fusion | flops 543686656 | bytes 2895360 | tf_op jit(solution)/shard_map/while/body/eval_jaxpr/dot_general | solution.py:89
  135.6 0.1 dynamic_slice.34
  135.7 15.3 %convolution_add_fusion.4 = f32[2048,128]{1,0:T(8,128)S(1)} fusion(bf16[128,2048]{1,0:T(8,128)(2,1)S(1)} %get-tuple-element.249, f32[2048]{0:T(1024)S(1)} %convert_element_type.131, f32[512]{0:T(512)S(1)} %dynamic_slice.34, f32[2048,128]{1,0:T(8,128)S(1)} %get-tuple-element.235, pred[]{:T(512)S(6)} %compare.3, ...), kind=kOutput, calls=%fused_computation.4.clone.1 | convolution fusion | flops 543686656 | bytes 2895360 | tf_op jit(solution)/shard_map/while/body/eval_jaxpr/dot_general | solution.py:89
  151.2 1.0 copy-done.2
  152.3 0.0 all-reduce.4.cloned.1.call-update
  152.3 3.9 fusion.10
  156.2 0.1 reshape.108
  156.3 0.1 fusion.37
  156.3 0.1 reshape.68
  156.4 0.1 fusion.36
  156.5 0.3 convolution_bitcast_fusion.5
  156.8 62.8 %psum.70 = f32[128]{0:T(128)S(1)} all-reduce(f32[128]{0:T(128)S(1)} %convolution_bitcast_fusion.5), channel_id=1, replica_groups=mesh['blk'=32,'col'=16] {'blk'}, use_global_device_ids=true, to_apply=%region_5.6 | all-reduce | flops 128 | bytes 1024 | tf_op jit(solution)/shard_map/psum | solution.py:96
  219.6 15.7 %all-gather = f32[16,1,128]{2,1,0:T(1,128)S(1)} all-gather(f32[1,1,128]{2,1,0:T(1,128)S(1)} %fusion.50), channel_id=1, replica_groups=mesh['blk'=32,'col'=16] {'col'}, dimensions={0}, use_global_device_ids=true | all-gather | bytes 8704 | tf_op jit(solution)/shard_map/all_gather | solution.py:104
  235.3 73.6 %all-reduce.4.cloned.1.call-done = f32[2048,128]{1,0:T(8,128)} async-done(((f32[2048,128]{1,0:T(8,128)}), f32[2048,128]{1,0:T(8,128)}) %all-reduce.4.cloned.1.call-update) | async-done | bytes 1048592 | tf_op jit(solution)/shard_map/psum | solution.py:96
  308.9 2.6 multiply_reduce_fusion.3
  311.5 24.8 %all-reduce.1 = (f32[]{:T(128)}, f32[]{:T(128)}) all-reduce(f32[]{:T(128)} %get-tuple-element.152, f32[]{:T(128)} %get-tuple-element.151), channel_id=1, replica_groups=mesh['blk'=32,'col'=16] {'col'}, use_global_device_ids=true, to_apply=%region_7.8 | all-reduce | flops 2 | bytes 16 | tf_op jit(solution)/shard_map/psum | solution.py:21
  337.6 0.6 multiply_reduce_fusion.2
  338.2 24.5 %psum.74 = f32[]{:T(128)} all-reduce(f32[]{:T(128)} %get-tuple-element.173), channel_id=1, replica_groups=mesh['blk'=32,'col'=16] {'col'}, use_global_device_ids=true, to_apply=%region_14.15 | all-reduce | flops 1 | bytes 8 | tf_op jit(solution)/shard_map/psum | solution.py:21
  364.1 14.4 %all-gather.2 = f32[16,1,128]{2,1,0:T(1,128)S(1)} all-gather(f32[1,1,128]{2,1,0:T(1,128)S(1)} %bitcast.116), channel_id=1, replica_groups=mesh['blk'=32,'col'=16] {'col'}, dimensions={0}, use_global_device_ids=true | all-gather | bytes 8704 | tf_op jit(solution)/shard_map/all_gather | solution.py:104
  378.5 1.2 multiply_reduce_fusion.1
  379.7 27.3 %psum.75 = f32[]{:T(128)} all-reduce(f32[]{:T(128)} %get-tuple-element.176), channel_id=1, replica_groups=mesh['blk'=32,'col'=16] {'col'}, use_global_device_ids=true, to_apply=%region_16.17 | all-reduce | flops 1 | bytes 8 | tf_op jit(solution)/shard_map/psum | solution.py:106
  408.3 0.6 multiply_reduce_fusion
  408.9 0.1 reshape.69
  409.0 24.2 %psum.76 = f32[]{:T(128)} all-reduce(f32[]{:T(128)} %multiply_reduce_fusion), channel_id=1, replica_groups=mesh['blk'=32,'col'=16] {'col'}, use_global_device_ids=true, to_apply=%region_18.19 | all-reduce | flops 1 | bytes 8 | tf_op jit(solution)/shard_map/psum | solution.py:21
  434.5 14.1 %all-gather.3 = f32[16,1,128]{2,1,0:T(1,128)S(1)} all-gather(f32[1,1,128]{2,1,0:T(1,128)S(1)} %bitcast.117), channel_id=1, replica_groups=mesh['blk'=32,'col'=16] {'col'}, dimensions={0}, use_global_device_ids=true | all-gather | bytes 8704 | tf_op jit(solution)/shard_map/all_gather | solution.py:104
  448.6 1.2 fusion.21
  449.8 26.1 %psum.77 = f32[]{:T(128)} all-reduce(f32[]{:T(128)} %fusion.21), channel_id=1, replica_groups=mesh['blk'=32,'col'=16] {'col'}, use_global_device_ids=true, to_apply=%region_20.21 | all-reduce | flops 1 | bytes 8 | tf_op jit(solution)/shard_map/psum | solution.py:106
  477.2 0.0 copy-start.5
  477.3 0.5 fusion.43
  477.8 0.5 fusion.45
  478.3 45.7 %all-reduce = (f32[2048]{0:T(1024)S(1)}, f32[2048]{0:T(1024)S(1)}) all-reduce(f32[2048]{0:T(1024)S(1)} %bitcast.112, f32[2048]{0:T(1024)S(1)} %bitcast.111), channel_id=1, replica_groups=mesh['blk'=32,'col'=16] {'col'}, use_global_device_ids=true, to_apply=%region_21.22 | all-reduce | flops 4096 | bytes 32768 | tf_op jit(solution)/shard_map/psum | solution.py:116
  524.0 0.1 reshape.67
  524.1 0.1 copy.26
  524.1 0.6 convolution_bitcast_fusion.4
  524.7 0.5 fusion.17
  525.2 0.1 exponential_reduce_fusion
  525.3 0.5 fusion.42
  (45 shorter events, 0.3 us)
Async XLA Ops:
  7.2 145.1 %copy-start = (bf16[128,16,128]{2,1,0:T(8,128)(2,1)S(1)}, bf16[128,16,128]{2,1,0:T(8,128)(2,1)}, u32[]{:S(2)}) copy-start(bf16[128,16,128]{2,1,0:T(8,128)(2,1)} %param.19) | copy-start | bytes 1572868
  7.2 10.3 %copy-start.3 = (s32[1024,1]{0,1:T(1,128)S(1)}, s32[1024,1]{0,1:T(1,128)}, u32[]{:S(2)}) copy-start(s32[1024,1]{0,1:T(1,128)} %param.15) | copy-start | bytes 12292
  7.2 10.3 %copy-start.6 = (s32[1024]{0:T(1024)S(1)}, s32[1024]{0:T(1024)}, u32[]{:S(2)}) copy-start(s32[1024]{0:T(1024)} %param.16) | copy-start | bytes 12292
  7.2 10.4 %copy-start.7 = (bf16[1024]{0:T(1024)(128)(2,1)S(1)}, bf16[1024]{0:T(1024)(128)(2,1)}, u32[]{:S(2)}) copy-start(bf16[1024]{0:T(1024)(128)(2,1)} %param.14) | copy-start | bytes 6148
  7.2 10.4 %copy-start.8 = (bf16[1024]{0:T(1024)(128)(2,1)S(1)}, bf16[1024]{0:T(1024)(128)(2,1)}, u32[]{:S(2)}) copy-start(bf16[1024]{0:T(1024)(128)(2,1)} %param.13) | copy-start | bytes 6148
  21.2 25.1 %copy-start.10 = (bf16[128]{0:T(256)(128)(2,1)S(1)}, bf16[128]{0:T(256)(128)(2,1)}, u32[]{:S(2)}) copy-start(bf16[128]{0:T(256)(128)(2,1)} %param.18) | copy-start | bytes 772
  21.2 48.2 %copy-start.4 = (bf16[128,128]{1,0:T(8,128)(2,1)S(1)}, bf16[128,128]{1,0:T(8,128)(2,1)}, u32[]{:S(2)}) copy-start(bf16[128,128]{1,0:T(8,128)(2,1)} %param.17) | copy-start | bytes 98308
  22.1 17.9 %all-to-all-start = ((bf16[32,3,64]{2,1,0:T(4,128)(2,1)}), bf16[32,3,64]{2,1,0:T(4,128)(2,1)S(1)}, u32[]{:S(2)}, u32[]{:S(2)}) async-start(bf16[32,3,64]{2,1,0:T(4,128)(2,1)} %bitcast.8), calls=%async_computation | async-start | bytes 65536 | tf_op jit(solution)/shard_map/all_to_all | solution.py:64
  40.0 45.5 %all-to-all-start.1 = ((bf16[32,64,128]{2,1,0:T(8,128)(2,1)}), bf16[32,64,128]{2,1,0:T(8,128)(2,1)S(1)}, u32[]{:S(2)}, u32[]{:S(2)}) async-start(bf16[32,64,128]{2,1,0:T(8,128)(2,1)} %bitcast.10), calls=%async_computation.1 | async-start | bytes 1048576 | tf_op jit(solution)/shard_map/all_to_all | solution.py:63
  46.3 262.7 %all-reduce.4.cloned.1.call-start = ((), (), s32[]{:S(2)}) async-start(), calls=%async_computation.2 | async-start | bytes 2097152 | tf_op jit(solution)/shard_map/psum | solution.py:96
  151.2 1.0 copy-start.2
  308.9 69.6 %copy-start.1 = (f32[2048,128]{1,0:T(8,128)S(1)}, f32[2048,128]{1,0:T(8,128)}, u32[]{:S(2)}) copy-start(f32[2048,128]{1,0:T(8,128)} %all-reduce.4.cloned.1.call-done) | copy-start | bytes 3145732
  449.8 75.4 %copy-start.9 = (f32[128]{0:T(128)S(1)}, f32[128]{0:T(128)}, u32[]{:S(2)}) copy-start(f32[128]{0:T(128)} %param.20) | copy-start | bytes 1540
  449.8 75.5 %copy-start.11 = (s32[128]{0:T(128)S(1)}, s32[128]{0:T(128)}, u32[]{:S(2)}) copy-start(s32[128]{0:T(128)} %param.21) | copy-start | bytes 1540
  477.2 48.6 %copy-start.5 = (f32[128]{0:T(128)}, f32[128]{0:T(128)S(1)}, u32[]{:S(2)}) copy-start(f32[128]{0:T(128)S(1)} %multiply_add_fusion.1) | copy-start | bytes 1540
Sparse Core Ops, SparseCore 0:
  152.4 156.4 all-reduce.3
where the time goes:
time: 533 us
  blocking collectives  318 us (60%)
  waiting for transfers between devices  77.2 us (14%)
  matrix products  76.3 us (14%)
  between operations  21.1 us (4%)
  starting transfers between devices  16.3 us (3%)
  other arithmetic  12 us (2%)
  local copies, waits for them, and re-layouts  10.9 us (2%)
    psum x1, waiting for transfers between devices, on_device(): gram, rhs = lax.psum((gram, rhs_local), 'blk')  73.6 us
    psum x3, blocking collectives, norm_of(): return lax.psum(jnp.sum(vector * vector), 'col')  73.4 us
    psum x1, blocking collectives, on_device(): gram, rhs = lax.psum((gram, rhs_local), 'blk')  62.8 us
    dot_general x4, matrix products, add_block(): lax.dot_general(weighted, rows_phi, (((0,), (0,)), ((), ())), preferred_e...  61.1 us
    psum x2, blocking collectives, on_device(): alpha = norm_now / lax.psum(jnp.sum(direction * image), 'col')  53.3 us
    psum x1, blocking collectives, on_device(): fitted, node_value = lax.psum((fit_part, node_part), 'col')  45.7 us
    all_gather x3, blocking collectives, on_device(): whole = lax.all_gather(direction, 'col', axis=0, tiled=True)  44.2 us
    all_gather x1, blocking collectives, on_device(): lax.all_gather(inducing_phase, 'col', axis=0, tiled=True)  23.1 us
  transfers between devices with their start and end apart: 3, of which 2 were waited for; matrix products, arithmetic and copies ran while one was open for 2% of the time, Pallas kernels for 0%

commit v1 on v0

--- a/solution.py
+++ b/solution.py
@@ -8,6 +8,27 @@
 SQRT_TWO = math.sqrt(2.0)
 LOG_SHAPE = math.log(1.5)
 LINK = 0.4
+
+
+def stages_all_choose(in_array):
+    clean = jax.lax.psum(1, "col")
+    extra, carry, step_out = (clean, jax.lax.axis_index("col"), in_array.shape[1])
+    history = [it * extra if t == 1 else it for t, it in enumerate(in_array.shape)]
+    current_block = lax.dynamic_update_slice_in_dim(
+        jnp.zeros(history, in_array.dtype), in_array, carry * step_out, axis=1
+    )
+    piece_now = q_next = in_array
+    for src_i in range(1, extra // 2 + 1):
+        piece_now = jax.lax.ppermute(piece_now, "col", [(t, (t + 1) % extra) for t in range(extra)])
+        current_block = lax.dynamic_update_slice_in_dim(
+            current_block, piece_now, (carry - src_i) % extra * step_out, axis=1
+        )
+        if 2 * src_i < extra:
+            q_next = jax.lax.ppermute(q_next, "col", [(t, (t - 1) % extra) for t in range(extra)])
+            current_block = lax.dynamic_update_slice_in_dim(
+                current_block, q_next, (carry + src_i) % extra * step_out, axis=1
+            )
+    return current_block
 
 
 def features(covariates, frequency, phases):
@@ -74,7 +95,7 @@
     local_cols = inducing_freq.shape[1]
     inducing = local_cols * lax.axis_size("col")
     freq_all, phase_all = (
-        lax.all_gather(inducing_freq, "col", axis=1, tiled=True),
+        stages_all_choose(inducing_freq),
         lax.all_gather(inducing_phase, "col", axis=0, tiled=True),
     )
     step_rows = min(512, row_count)

time: 533 us -> 551 us (1.034)
  starting transfers between devices: 16.3 us -> 46.7 us
  blocking collectives: 318 us -> 294 us
  waiting for transfers between devices: 77.2 us -> 88.2 us
    ppermute x0 -> x15, starting transfers between devices: none -> 26.8 us  [the longest x7 26.8 us: stages_all_choose(): jax.lax.ppermute(q_next, 'col', [(t, (t - 1) % extra) for t in range(extr...]
    all_gather x1 -> x0, blocking collectives: 15.9 us -> none  [on_device(): lax.all_gather(inducing_freq, 'col', axis=1, tiled=True)]
    ppermute x0 -> x15, waiting for transfers between devices: none -> 13.3 us  [the longest x8 10.6 us: stages_all_choose(): jax.lax.ppermute(piece_now, 'col', [(t, (t + 1) % extra) for t in range(e...]
    all_gather x1, blocking collectives: 23.1 us -> 16.3 us  [on_device(): lax.all_gather(inducing_phase, 'col', axis=0, tiled=True)]
  transfers between devices with their start and end apart: 3 -> 18, of which waited for: 2 -> 13; matrix products, arithmetic and copies ran while one was open for 2% -> 4% of each run, Pallas kernels for 0% -> 0%
where the time goes in v1:
time: 551 us; the launch traced here: 550 us
  blocking collectives  294 us (53%)
  waiting for transfers between devices  88.2 us (16%)
  matrix products  76.3 us (14%)
  starting transfers between devices  46.7 us (8%)
  between operations  21.4 us (4%)
  other arithmetic  12 us (2%)
  local copies, waits for them, and re-layouts  11.2 us (2%)
    psum x1, waiting for transfers between devices, on_device(): gram, rhs = lax.psum((gram, rhs_local), 'blk')  74.9 us
    psum x3, blocking collectives, norm_of(): return lax.psum(jnp.sum(vector * vector), 'col')  73.4 us
    psum x1, blocking collectives, on_device(): gram, rhs = lax.psum((gram, rhs_local), 'blk')  62.8 us
    dot_general x4, matrix products, add_block(): lax.dot_general(weighted, rows_phi, (((0,), (0,)), ((), ())), preferred_e...  61 us
    psum x2, blocking collectives, on_device(): alpha = norm_now / lax.psum(jnp.sum(direction * image), 'col')  53.3 us
    psum x1, blocking collectives, on_device(): fitted, node_value = lax.psum((fit_part, node_part), 'col')  45.7 us
    all_gather x3, blocking collectives, on_device(): whole = lax.all_gather(direction, 'col', axis=0, tiled=True)  42.5 us
    ppermute x7, starting transfers between devices, stages_all_choose(): jax.lax.ppermute(q_next, 'col', [(t, (t - 1) % extra) for t in range(extr...  26.8 us
  transfers between devices with their start and end apart: 18, of which 13 were waited for; matrix products, arithmetic and copies ran while one was open for 4% of the time, Pallas kernels for 0%

profile of v1, /device:TPU:16, one launch (start us, length us, event | category | flops | bytes accessed | tf_op | source)
XLA Modules:
  0.0 550.4 jit_solution(13952724035080756659)
XLA Ops:
  7.2 8.5 %collective-permute-start.1 = (bf16[128,128]{1,0:T(8,128)(2,1)}, bf16[128,128]{1,0:T(8,128)(2,1)S(1)}, u32[]{:S(2)}, u32[]{:S(2)}) collective-permute-start(bf16[128,128]{1,0:T(8,128)(2,1)} %param.17), channel_id=1, source_target_pairs={{0,15},{1,0},{2,1},{3,2},{4,3},{5,4},{6,5},{7,6},{8,7},{9,8},{10,9... | collective-permute-start | bytes 98312 | tf_op jit(solution)/shard_map/ppermute | solution.py:27
  15.7 0.7 fusion.35
  16.4 9.0 %reduce-window.6 = s32[32,8,128]{2,1,0:T(8,128)S(1)} reduce-window(s32[32,8,128]{2,1,0:T(8,128)S(1)} %fusion.35, s32[]{:T(128)} %constant.160.clone.1), window={size=1x1x128 pad=0_0x0_0x127_0}, to_apply=%region_0.0 | reduce-window | flops 4161536 | bytes 262148 | tf_op jit(solution)/shard_map/reduce-window
  25.5 0.1 slice.24
  25.6 0.1 copy.22
  25.8 0.1 add_add_fusion
  26.1 0.2 copy.24
  26.3 3.3 scatter_custom_fusion
  29.7 0.9 copy.25
  30.5 10.1 %all-to-all-start = ((bf16[32,3,64]{2,1,0:T(4,128)(2,1)}), bf16[32,3,64]{2,1,0:T(4,128)(2,1)S(1)}, u32[]{:S(2)}, u32[]{:S(2)}) async-start(bf16[32,3,64]{2,1,0:T(4,128)(2,1)} %bitcast.8), calls=%async_computation | async-start | bytes 65536 | tf_op jit(solution)/shard_map/all_to_all | solution.py:85
  41.0 4.3 scatter_custom_fusion.1
  45.3 16.3 %all-gather.1 = bf16[16,1,128]{2,1,0:T(2,128)(2,1)S(1)} all-gather(bf16[1,1,128]{2,1,0:T(2,128)(2,1)S(1)} %bitcast.121), channel_id=1, replica_groups=mesh['blk'=32,'col'=16] {'col'}, dimensions={0}, use_global_device_ids=true | all-gather | bytes 4352 | tf_op jit(solution)/shard_map/all_gather | solution.py:99
  61.6 9.8 %all-to-all-start.1 = ((bf16[32,64,128]{2,1,0:T(8,128)(2,1)}), bf16[32,64,128]{2,1,0:T(8,128)(2,1)S(1)}, u32[]{:S(2)}, u32[]{:S(2)}) async-start(bf16[32,64,128]{2,1,0:T(8,128)(2,1)} %bitcast.10), calls=%async_computation.1 | async-start | bytes 1048576 | tf_op jit(solution)/shard_map/all_to_all | solution.py:84
  71.5 0.1 reshape_squeeze.2
  71.6 2.9 collective-permute-start.3
  74.6 1.6 collective-permute-done.2
  76.2 3.2 collective-permute-start.5
  79.5 1.3 collective-permute-done.4
  80.7 0.3 collective-permute-done.5
  81.0 3.2 collective-permute-start.7
  84.3 1.0 collective-permute-done.6
  85.3 0.6 collective-permute-done.7
  85.9 3.0 collective-permute-start.9
  88.9 1.0 collective-permute-done.8
  89.8 0.6 collective-permute-done.9
  90.4 3.0 collective-permute-start.11
  93.4 1.0 collective-permute-done.10
  94.4 0.6 collective-permute-done.11
  95.0 3.0 collective-permute-start.13
  98.0 1.0 collective-permute-done.12
  98.9 0.6 collective-permute-done.13
  99.5 3.9 collective-permute-done.14
  103.5 3.9 fusion.11
  107.4 61.9 %while.14 = (s32[]{:T(128)}, f32[2048,128]{1,0:T(8,128)S(1)}, f32[2048]{0:T(1024)S(1)}, bf16[2048,128]{1,0:T(8,128)(2,1)S(1)}, bf16[128,2048]{1,0:T(8,128)(2,1)S...) while((s32[]{:T(128)}, f32[2048,128]{1,0:T(8,128)S(1)}, ...), condition=%wide.region_9.10_spmd.clone, body=%wide.region_8.9_spmd.clone.sunk | while | flops 543688704 | bytes 2911912 | solution.py:114
  107.7 15.2 %convolution_add_fusion.4 = f32[2048,128]{1,0:T(8,128)S(1)} fusion(bf16[128,2048]{1,0:T(8,128)(2,1)S(1)} %get-tuple-element.249, f32[2048]{0:T(1024)S(1)} %convert_element_type.131, f32[512]{0:T(512)S(1)} %dynamic_slice.34, f32[2048,128]{1,0:T(8,128)S(1)} %get-tuple-element.235, pred[]{:T(512)S(6)} %compare.18, ...), kind=kOutput, calls=%fused_computation.4.clone.1 | convolution fusion | flops 543686656 | bytes 2895360 | tf_op jit(solution)/shard_map/while/body/eval_jaxpr/dot_general | solution.py:110
  123.0 15.3 %convolution_add_fusion.4 = f32[2048,128]{1,0:T(8,128)S(1)} fusion(bf16[128,2048]{1,0:T(8,128)(2,1)S(1)} %get-tuple-element.249, f32[2048]{0:T(1024)S(1)} %convert_element_type.131, f32[512]{0:T(512)S(1)} %dynamic_slice.34, f32[2048,128]{1,0:T(8,128)S(1)} %get-tuple-element.235, pred[]{:T(512)S(6)} %compare.18, ...), kind=kOutput, calls=%fused_computation.4.clone.1 | convolution fusion | flops 543686656 | bytes 2895360 | tf_op jit(solution)/shard_map/while/body/eval_jaxpr/dot_general | solution.py:110
  138.4 15.3 %convolution_add_fusion.4 = f32[2048,128]{1,0:T(8,128)S(1)} fusion(bf16[128,2048]{1,0:T(8,128)(2,1)S(1)} %get-tuple-element.249, f32[2048]{0:T(1024)S(1)} %convert_element_type.131, f32[512]{0:T(512)S(1)} %dynamic_slice.34, f32[2048,128]{1,0:T(8,128)S(1)} %get-tuple-element.235, pred[]{:T(512)S(6)} %compare.18, ...), kind=kOutput, calls=%fused_computation.4.clone.1 | convolution fusion | flops 543686656 | bytes 2895360 | tf_op jit(solution)/shard_map/while/body/eval_jaxpr/dot_general | solution.py:110
  153.8 15.3 %convolution_add_fusion.4 = f32[2048,128]{1,0:T(8,128)S(1)} fusion(bf16[128,2048]{1,0:T(8,128)(2,1)S(1)} %get-tuple-element.249, f32[2048]{0:T(1024)S(1)} %convert_element_type.131, f32[512]{0:T(512)S(1)} %dynamic_slice.34, f32[2048,128]{1,0:T(8,128)S(1)} %get-tuple-element.235, pred[]{:T(512)S(6)} %compare.18, ...), kind=kOutput, calls=%fused_computation.4.clone.1 | convolution fusion | flops 543686656 | bytes 2895360 | tf_op jit(solution)/shard_map/while/body/eval_jaxpr/dot_general | solution.py:110
  169.3 1.0 copy-done.2
  170.3 3.9 fusion.10
  174.2 0.1 reshape.108
  174.5 0.3 convolution_bitcast_fusion.5
  174.8 62.8 %psum.70 = f32[128]{0:T(128)S(1)} all-reduce(f32[128]{0:T(128)S(1)} %convolution_bitcast_fusion.5), channel_id=1, replica_groups=mesh['blk'=32,'col'=16] {'blk'}, use_global_device_ids=true, to_apply=%region_5.6 | all-reduce | flops 128 | bytes 1024 | tf_op jit(solution)/shard_map/psum | solution.py:117
  237.7 14.0 %all-gather = f32[16,1,128]{2,1,0:T(1,128)S(1)} all-gather(f32[1,1,128]{2,1,0:T(1,128)S(1)} %fusion.50), channel_id=1, replica_groups=mesh['blk'=32,'col'=16] {'col'}, dimensions={0}, use_global_device_ids=true | all-gather | bytes 8704 | tf_op jit(solution)/shard_map/all_gather | solution.py:125
  251.7 74.9 %all-reduce.4.cloned.1.call-done = f32[2048,128]{1,0:T(8,128)} async-done(((f32[2048,128]{1,0:T(8,128)}), f32[2048,128]{1,0:T(8,128)}) %all-reduce.4.cloned.1.call-update) | async-done | bytes 1048592 | tf_op jit(solution)/shard_map/psum | solution.py:117
  326.6 2.6 multiply_reduce_fusion.3
  329.2 24.8 %all-reduce.1 = (f32[]{:T(128)}, f32[]{:T(128)}) all-reduce(f32[]{:T(128)} %get-tuple-element.152, f32[]{:T(128)} %get-tuple-element.151), channel_id=1, replica_groups=mesh['blk'=32,'col'=16] {'col'}, use_global_device_ids=true, to_apply=%region_7.8 | all-reduce | flops 2 | bytes 16 | tf_op jit(solution)/shard_map/psum | solution.py:42
  355.3 0.6 multiply_reduce_fusion.2
  355.9 24.5 %psum.74 = f32[]{:T(128)} all-reduce(f32[]{:T(128)} %get-tuple-element.173), channel_id=1, replica_groups=mesh['blk'=32,'col'=16] {'col'}, use_global_device_ids=true, to_apply=%region_14.15 | all-reduce | flops 1 | bytes 8 | tf_op jit(solution)/shard_map/psum | solution.py:42
  381.8 14.4 %all-gather.2 = f32[16,1,128]{2,1,0:T(1,128)S(1)} all-gather(f32[1,1,128]{2,1,0:T(1,128)S(1)} %bitcast.116), channel_id=1, replica_groups=mesh['blk'=32,'col'=16] {'col'}, dimensions={0}, use_global_device_ids=true | all-gather | bytes 8704 | tf_op jit(solution)/shard_map/all_gather | solution.py:125
  396.2 1.2 multiply_reduce_fusion.1
  397.4 27.3 %psum.75 = f32[]{:T(128)} all-reduce(f32[]{:T(128)} %get-tuple-element.176), channel_id=1, replica_groups=mesh['blk'=32,'col'=16] {'col'}, use_global_device_ids=true, to_apply=%region_16.17 | all-reduce | flops 1 | bytes 8 | tf_op jit(solution)/shard_map/psum | solution.py:127
  426.0 0.6 multiply_reduce_fusion
  426.7 24.2 %psum.76 = f32[]{:T(128)} all-reduce(f32[]{:T(128)} %multiply_reduce_fusion), channel_id=1, replica_groups=mesh['blk'=32,'col'=16] {'col'}, use_global_device_ids=true, to_apply=%region_18.19 | all-reduce | flops 1 | bytes 8 | tf_op jit(solution)/shard_map/psum | solution.py:42
  452.2 14.1 %all-gather.3 = f32[16,1,128]{2,1,0:T(1,128)S(1)} all-gather(f32[1,1,128]{2,1,0:T(1,128)S(1)} %bitcast.117), channel_id=1, replica_groups=mesh['blk'=32,'col'=16] {'col'}, dimensions={0}, use_global_device_ids=true | all-gather | bytes 8704 | tf_op jit(solution)/shard_map/all_gather | solution.py:125
  466.3 1.2 fusion.21
  467.5 26.1 %psum.77 = f32[]{:T(128)} all-reduce(f32[]{:T(128)} %fusion.21), channel_id=1, replica_groups=mesh['blk'=32,'col'=16] {'col'}, use_global_device_ids=true, to_apply=%region_20.21 | all-reduce | flops 1 | bytes 8 | tf_op jit(solution)/shard_map/psum | solution.py:127
  494.9 0.5 fusion.43
  495.5 0.5 fusion.45
  496.0 45.7 %all-reduce = (f32[2048]{0:T(1024)S(1)}, f32[2048]{0:T(1024)S(1)}) all-reduce(f32[2048]{0:T(1024)S(1)} %bitcast.112, f32[2048]{0:T(1024)S(1)} %bitcast.111), channel_id=1, replica_groups=mesh['blk'=32,'col'=16] {'col'}, use_global_device_ids=true, to_apply=%region_21.22 | all-reduce | flops 4096 | bytes 32768 | tf_op jit(solution)/shard_map/psum | solution.py:137
  541.8 0.6 convolution_bitcast_fusion.4
  542.4 0.5 fusion.17
  542.9 0.1 exponential_reduce_fusion
  543.0 0.5 fusion.42
  (91 shorter events, 1.5 us)
Async XLA Ops:
  7.2 163.2 %copy-start = (bf16[128,16,128]{2,1,0:T(8,128)(2,1)S(1)}, bf16[128,16,128]{2,1,0:T(8,128)(2,1)}, u32[]{:S(2)}) copy-start(bf16[128,16,128]{2,1,0:T(8,128)(2,1)} %param.19) | copy-start | bytes 1572868
  7.2 18.7 %copy-start.3 = (s32[1024,1]{0,1:T(1,128)S(1)}, s32[1024,1]{0,1:T(1,128)}, u32[]{:S(2)}) copy-start(s32[1024,1]{0,1:T(1,128)} %param.15) | copy-start | bytes 12292
  7.2 18.8 %copy-start.6 = (s32[1024]{0:T(1024)S(1)}, s32[1024]{0:T(1024)}, u32[]{:S(2)}) copy-start(s32[1024]{0:T(1024)} %param.16) | copy-start | bytes 12292
  7.2 18.8 %copy-start.7 = (bf16[1024]{0:T(1024)(128)(2,1)S(1)}, bf16[1024]{0:T(1024)(128)(2,1)}, u32[]{:S(2)}) copy-start(bf16[1024]{0:T(1024)(128)(2,1)} %param.14) | copy-start | bytes 6148
  7.2 18.8 %copy-start.8 = (bf16[1024]{0:T(1024)(128)(2,1)S(1)}, bf16[1024]{0:T(1024)(128)(2,1)}, u32[]{:S(2)}) copy-start(bf16[1024]{0:T(1024)(128)(2,1)} %param.13) | copy-start | bytes 6148
  7.2 64.4 %collective-permute-start = (bf16[128,128]{1,0:T(8,128)(2,1)}, bf16[128,128]{1,0:T(8,128)(2,1)S(1)}, u32[]{:S(2)}, u32[]{:S(2)}) collective-permute-start(bf16[128,128]{1,0:T(8,128)(2,1)} %param.17), channel_id=1, source_target_pairs={{0,1},{1,2},{2,3},{3,4},{4,5},{5,6},{6,7},{7,8},{8,9},{9,10},{10,1... | collective-permute-start | bytes 98312 | tf_op jit(solution)/shard_map/ppermute | solution.py:22
  7.2 64.4 %collective-permute-start.1 = (bf16[128,128]{1,0:T(8,128)(2,1)}, bf16[128,128]{1,0:T(8,128)(2,1)S(1)}, u32[]{:S(2)}, u32[]{:S(2)}) collective-permute-start(bf16[128,128]{1,0:T(8,128)(2,1)} %param.17), channel_id=1, source_target_pairs={{0,15},{1,0},{2,1},{3,2},{4,3},{5,4},{6,5},{7,6},{8,7},{9,8},{10,9... | collective-permute-start | bytes 98312 | tf_op jit(solution)/shard_map/ppermute | solution.py:27
  25.9 14.7 %copy-start.4 = (bf16[128,128]{1,0:T(8,128)(2,1)S(1)}, bf16[128,128]{1,0:T(8,128)(2,1)}, u32[]{:S(2)}) copy-start(bf16[128,128]{1,0:T(8,128)(2,1)} %param.17) | copy-start | bytes 98308
  29.7 15.6 %copy-start.10 = (bf16[128]{0:T(256)(128)(2,1)S(1)}, bf16[128]{0:T(256)(128)(2,1)}, u32[]{:S(2)}) copy-start(bf16[128]{0:T(256)(128)(2,1)} %param.18) | copy-start | bytes 772
  30.5 31.1 %all-to-all-start = ((bf16[32,3,64]{2,1,0:T(4,128)(2,1)}), bf16[32,3,64]{2,1,0:T(4,128)(2,1)S(1)}, u32[]{:S(2)}, u32[]{:S(2)}) async-start(bf16[32,3,64]{2,1,0:T(4,128)(2,1)} %bitcast.8), calls=%async_computation | async-start | bytes 65536 | tf_op jit(solution)/shard_map/all_to_all | solution.py:85
  61.6 41.9 %all-to-all-start.1 = ((bf16[32,64,128]{2,1,0:T(8,128)(2,1)}), bf16[32,64,128]{2,1,0:T(8,128)(2,1)S(1)}, u32[]{:S(2)}, u32[]{:S(2)}) async-start(bf16[32,64,128]{2,1,0:T(8,128)(2,1)} %bitcast.10), calls=%async_computation.1 | async-start | bytes 1048576 | tf_op jit(solution)/shard_map/all_to_all | solution.py:84
  71.4 255.2 %all-reduce.4.cloned.1.call-start = ((), (), s32[]{:S(2)}) async-start(), calls=%async_computation.2 | async-start | bytes 2097152 | tf_op jit(solution)/shard_map/psum | solution.py:117
  71.6 4.6 collective-permute-start.2
  71.6 4.5 collective-permute-start.3
  76.2 4.6 collective-permute-start.4
  76.2 4.8 collective-permute-start.5
  80.7 4.6 collective-permute-start.6
  81.0 4.8 collective-permute-start.7
  85.3 4.6 collective-permute-start.8
  85.9 4.6 collective-permute-start.9
  89.8 4.6 collective-permute-start.10
  90.4 4.6 collective-permute-start.11
  94.4 4.6 collective-permute-start.12
  95.0 4.6 collective-permute-start.13
  98.9 4.6 collective-permute-start.14
  169.3 1.0 copy-start.2
  326.6 69.6 %copy-start.1 = (f32[2048,128]{1,0:T(8,128)S(1)}, f32[2048,128]{1,0:T(8,128)}, u32[]{:S(2)}) copy-start(f32[2048,128]{1,0:T(8,128)} %all-reduce.4.cloned.1.call-done) | copy-start | bytes 3145732
  467.5 75.4 %copy-start.9 = (f32[128]{0:T(128)S(1)}, f32[128]{0:T(128)}, u32[]{:S(2)}) copy-start(f32[128]{0:T(128)} %param.20) | copy-start | bytes 1540
  467.5 75.5 %copy-start.11 = (s32[128]{0:T(128)S(1)}, s32[128]{0:T(128)}, u32[]{:S(2)}) copy-start(s32[128]{0:T(128)} %param.21) | copy-start | bytes 1540
  494.9 48.6 %copy-start.5 = (f32[128]{0:T(128)}, f32[128]{0:T(128)S(1)}, u32[]{:S(2)}) copy-start(f32[128]{0:T(128)S(1)} %multiply_add_fusion.1) | copy-start | bytes 1540
Sparse Core Ops, SparseCore 0:
  170.5 156.1 all-reduce.3
